TPU v7x, 512 devices: a whole 4x8x8 slice. The times are simulated.
512 devices in a mesh: ctx: 16 (over y, core), enc: 32 (over z, x).
Axes of the slice: x: 4, y: 8, z: 8, core: 2. Of those that a mesh axis runs over, the one named last changes fastest.
Arguments:
- queries: bfloat16 [32, 2048, 4096], P('enc', 'ctx'), may hold values from -200 to 200
- d_out: bfloat16 [32, 2048, 4096], P('enc', 'ctx'), may hold values from -24 to 24
- text_sample: int32 [32, 2048], P('enc', 'ctx'), may hold values from 0 to 1, as said below
- tiles: int32 [32, 2], P('enc'), may hold values from 1 to 4
- img_k: bfloat16 [32, 512, 1024], P(None, ('ctx', 'enc')), may hold values from -20 to 20
- img_v: bfloat16 [32, 512, 1024], P(None, ('ctx', 'enc')), may hold values from -6 to 6
Outputs:
- d_queries: bfloat16 [32, 2048, 4096], P('enc', 'ctx')
- d_img_k: bfloat16 [32, 512, 1024], P(None, ('ctx', 'enc'))
- d_img_v: bfloat16 [32, 512, 1024], P(None, ('ctx', 'enc'))
Inputs may be any that keep to these rules, and one draw needn't show every extreme that they name: `text_sample`: within each group the sample numbers never fall along the text, and each of the 2 samples has at least one token.
All inputs are finite; a program needn't handle non-finite values.
Results may differ from a plain program's by a relative error of at most 0.022.
Values may be sent and summed in bfloat16 or wider, within the bound.
A program may use at most 128 MiB of HBM per device.

v0:
```python
import jax
import jax.numpy as jnp
from jax import lax
from jax.sharding import PartitionSpec as P

H = 32
KVH = 8
HD = 128
SAMP = 2
MAX_TILES = 4
TILE_TOK = 64


big_negative = -1e30


def key_allowed(token_sample, tile_row, slot_count):
    slot_rows = MAX_TILES * TILE_TOK
    key_index = jnp.arange(slot_count, dtype=jnp.int32)
    key_sample = key_index // slot_rows
    key_tile = key_index % slot_rows // TILE_TOK
    matches = key_sample[:, None] == jnp.arange(SAMP, dtype=jnp.int32)[None, :]
    limit = jnp.sum(jnp.where(matches, tile_row[None, :], 0), axis=1)
    valid = key_tile < limit
    return (token_sample[:, None] == key_sample[None, :]) & valid[None, :]


def shards(queries, d_out, text_sample, tiles, img_k, img_v):
    group_ratio = H // KVH
    score_scale = HD ** (-0.5)
    token_count = queries.shape[1]
    query_heads = queries[0].reshape(token_count, KVH, group_ratio, HD)
    grad_heads = d_out[0].reshape(token_count, KVH, group_ratio, HD)
    token_sample = text_sample[0]
    tile_row = tiles[0]
    own_keys, own_values = (
        lax.all_to_all(img_k, "enc", split_axis=0, concat_axis=1, tiled=True),
        lax.all_to_all(img_v, "enc", split_axis=0, concat_axis=1, tiled=True),
    )
    own_keys = own_keys[0]
    own_values = own_values[0]
    all_keys, all_values = (
        lax.all_gather(own_keys, "ctx", axis=0, tiled=True),
        lax.all_gather(own_values, "ctx", axis=0, tiled=True),
    )
    block_rows = all_keys.shape[0]
    key_heads = all_keys.reshape(block_rows, KVH, HD)
    scores = (
        jnp.einsum("tagd,kad->agtk", query_heads, key_heads, preferred_element_type=jnp.float32)
        * score_scale
    )
    allowed = key_allowed(token_sample, tile_row, block_rows)
    scores, allowed, key_heads = (jnp.where(allowed, scores, big_negative), allowed, key_heads)
    row_max = jnp.max(scores, axis=-1)
    weights = jnp.where(allowed, jnp.exp(scores - row_max[..., None]), 0.0)
    log_total = row_max + jnp.log(jnp.sum(weights, axis=-1))
    probs = jnp.where(allowed, jnp.exp(scores - log_total[..., None]), 0.0)
    value_heads = all_values.reshape(all_values.shape[0], KVH, HD)
    grad_probs = jnp.einsum(
        "tagd,kad->agtk", grad_heads, value_heads, preferred_element_type=jnp.float32
    )
    row_dot = jnp.sum(probs * grad_probs, axis=-1)
    grad_scores = (probs * (grad_probs - row_dot[..., None]) * score_scale).astype(jnp.bfloat16)
    probs_half = probs.astype(jnp.bfloat16)
    query_part = jnp.einsum(
        "agtk,kad->tagd", grad_scores, key_heads, preferred_element_type=jnp.float32
    )
    key_part = jnp.einsum(
        "agtk,tagd->kad", grad_scores, query_heads, preferred_element_type=jnp.float32
    )
    value_part = jnp.einsum(
        "agtk,tagd->kad", probs_half, grad_heads, preferred_element_type=jnp.float32
    )
    block_rows = key_heads.shape[0]
    grad_key_all = key_part.reshape(block_rows, KVH * HD)
    grad_value_all = value_part.reshape(block_rows, KVH * HD)
    key_sums, value_sums = (
        lax.psum_scatter(
            grad_key_all.astype(jnp.bfloat16), "ctx", scatter_dimension=0, tiled=True
        ).astype(jnp.float32),
        lax.psum_scatter(
            grad_value_all.astype(jnp.bfloat16), "ctx", scatter_dimension=0, tiled=True
        ).astype(jnp.float32),
    )
    back_keys, back_values = (
        lax.all_to_all(
            key_sums.astype(jnp.bfloat16)[None], "enc", split_axis=1, concat_axis=0, tiled=True
        ),
        lax.all_to_all(
            value_sums.astype(jnp.bfloat16)[None], "enc", split_axis=1, concat_axis=0, tiled=True
        ),
    )
    d_queries = query_part.reshape(1, token_count, H * HD).astype(jnp.bfloat16)
    return (d_queries, back_keys, back_values)


def solution(mesh):
    in_specs = (
        P("enc", "ctx", None),
        P("enc", "ctx", None),
        P("enc", "ctx"),
        P("enc", None),
        P(None, ("ctx", "enc"), None),
        P(None, ("ctx", "enc"), None),
    )
    out_specs = (
        P("enc", "ctx", None),
        P(None, ("ctx", "enc"), None),
        P(None, ("ctx", "enc"), None),
    )
    return jax.shard_map(shards, mesh=mesh, in_specs=in_specs, out_specs=out_specs, check_vma=False)
```

profile of v0, /device:TPU:1, one launch (start us, length us, event | category | flops | bytes accessed | tf_op | source)
XLA Modules:
  0.0 268.6 jit_solution(4134127797427280373)
XLA Ops:
  7.7 1.5 reduce
  9.3 22.3 %all_to_all.42 = bf16[32,2,512]{2,1,0:T(2,128)(2,1)S(1)} all-to-all(bf16[32,2,512]{2,1,0:T(2,128)(2,1)S(1)} %reshape.117), channel_id=1, replica_groups=mesh['ctx'=16,'enc'=32] {'enc'}, dimensions={0} | all-to-all | bytes 131072 | tf_op jit(solution)/shard_map/all_to_all | solution.py:37
  32.3 1.5 reduce.1
  33.8 0.7 reshape.119
  34.5 3.9 %all-to-all-start.1 = ((bf16[32,2,512]{2,1,0:T(2,128)(2,1)}), bf16[32,2,512]{2,1,0:T(2,128)(2,1)S(1)}, u32[]{:S(2)}, u32[]{:S(2)}) async-start(bf16[32,2,512]{2,1,0:T(2,128)(2,1)} %reshape.119), calls=%async_computation.1 | async-start | bytes 131072 | tf_op jit(solution)/shard_map/all_to_all | solution.py:38
  38.4 1.6 copy.106
  40.0 1.6 copy.107
  41.7 0.7 fusion.13
  42.4 0.9 compare_and_fusion
  43.3 4.0 %all-to-all-done.1 = bf16[32,2,512]{2,1,0:T(2,128)(2,1)S(1)} async-done(((bf16[32,2,512]{2,1,0:T(2,128)(2,1)}), bf16[32,2,512]{2,1,0:T(2,128)(2,1)S(1)}, u32[]{:S(2)}, u32[]{:S(2)}) %all-to-all-start.1) | async-done | bytes 65568 | tf_op jit(solution)/shard_map/all_to_all | solution.py:38
  48.0 22.0 %all-gather.5.cloned.1.call-done = bf16[512,1,1024]{2,0,1:T(8,128)(2,1)} async-done(((bf16[32,1,1024]{2,0,1:T(8,128)(2,1)}), bf16[512,1,1024]{2,0,1:T(8,128)(2,1)}) %all-gather.5.cloned.1.call-update) | async-done | bytes 1048592 | tf_op jit(solution)/shard_map/all_gather | solution.py:43
  70.0 1.5 copy.74
  71.5 1.4 fusion.4
  72.9 2.1 select_reduce_fusion
  75.0 3.2 %bitcast_convert_fusion = bf16[8,512,128]{1,2,0:T(8,128)(2,1)} fusion(bf16[128,8,4,128]{0,3,2,1:T(8,128)(2,1)S(1)} %bitcast.119, f32[8,512,128,4]{2,1,3,0:T(8,128)S(1)} %get-tuple-element.19, f32[8,4,128]{2,1,0:T(4,128)S(1)} %bitcast.135, pred[128,512]{0,1:T(8,128)(4,1)S(1)} %compare_and_fusion), kind=kOutput, calls=%fused_computation.15 | convolution fusion | flops 547880960 | bytes 10567680 | tf_op jit(solution)/shard_map/agtk,tagd->kad/dot_general | solution.py:71
  78.2 2.3 copy.89
  80.7 31.9 %all-gather.7.cloned.1.call-done = bf16[512,1,1024]{2,0,1:T(8,128)(2,1)} async-done(((bf16[32,1,1024]{2,0,1:T(8,128)(2,1)}), bf16[512,1,1024]{2,0,1:T(8,128)(2,1)}) %all-gather.7.cloned.1.call-update) | async-done | bytes 1048592 | tf_op jit(solution)/shard_map/all_gather | solution.py:44
  112.6 2.3 copy.79
  114.9 5.7 %fusion.39 = f32[8,512,128,4]{2,1,3,0:T(8,128)} fusion(bf16[512,8,128,1]{0,2,3,1:T(8,128)(2,1)} %bitcast.121, bf16[128,8,4,128]{0,3,2,1:T(8,128)(2,1)S(1)} %bitcast.120), kind=kOutput, calls=%fused_computation.54 | convolution fusion | flops 536870912 | bytes 10485760 | tf_op jit(solution)/shard_map/tagd,kad->agtk/dot_general | solution.py:59
  120.6 13.7 %bitcast_convert_fusion.1 = bf16[8,512,128]{1,2,0:T(8,128)(2,1)S(1)} fusion(bf16[128,8,4,128]{0,3,2,1:T(8,128)(2,1)S(1)} %bitcast.118, f32[8,512,128,4]{2,1,3,0:T(8,128)} %fusion.39, f32[8,512,128,4]{2,1,3,0:T(8,128)} %copy-done, f32[8,4,128]{2,1,0:T(4,128)S(1)} %bitcast.136, pred[128,512]{0,1:T(8,128)(4,1)S(1)} %compare_and_fusion), kind=kOutput, calls=%fused_computation.16 | convolution fusion | flops 564662784 | bytes 18956288 | tf_op jit(solution)/shard_map/agtk,tagd->kad/dot_general | solution.py:68
  134.3 1.3 copy.85
  135.7 36.5 %reduce-scatter.5.cloned.1.call-done = bf16[32,1024]{1,0:T(8,128)(2,1)} async-done(((bf16[512,1024]{1,0:T(8,128)(2,1)}), bf16[32,1024]{1,0:T(8,128)(2,1)}) %reduce-scatter.5.cloned.1.call-update) | async-done | bytes 65552 | tf_op jit(solution)/shard_map/reduce_scatter | solution.py:81
  172.1 0.9 copy.114
  173.1 1.0 reduce.3
  174.1 0.7 reshape.123
  174.7 8.8 %all-to-all-start.3 = ((bf16[32,2,512]{2,1,0:T(2,128)(2,1)}), bf16[32,2,512]{2,1,0:T(2,128)(2,1)S(1)}, u32[]{:S(2)}, u32[]{:S(2)}) async-start(bf16[32,2,512]{2,1,0:T(2,128)(2,1)} %reshape.123), calls=%async_computation.5 | async-start | bytes 131072 | tf_op jit(solution)/shard_map/all_to_all | solution.py:89
  183.5 51.1 %reduce-scatter.3.cloned.1.call-done = bf16[32,1024]{1,0:T(8,128)(2,1)} async-done(((bf16[512,1024]{1,0:T(8,128)(2,1)}), bf16[32,1024]{1,0:T(8,128)(2,1)}) %reduce-scatter.3.cloned.1.call-update) | async-done | bytes 65552 | tf_op jit(solution)/shard_map/reduce_scatter | solution.py:78
  234.6 0.9 copy.115
  235.6 1.0 reduce.2
  237.2 8.5 %all-to-all-start.2 = ((bf16[32,2,512]{2,1,0:T(2,128)(2,1)}), bf16[32,2,512]{2,1,0:T(2,128)(2,1)S(1)}, u32[]{:S(2)}, u32[]{:S(2)}) async-start(bf16[32,2,512]{2,1,0:T(2,128)(2,1)} %reshape.121), calls=%async_computation.3 | async-start | bytes 131072 | tf_op jit(solution)/shard_map/all_to_all | solution.py:86
  245.8 13.5 %fusion.12 = bf16[8,4,128,128]{2,3,1,0:T(8,128)(2,1)S(1)} fusion(bf16[512,8,128,1]{0,2,3,1:T(8,128)(2,1)S(1)} %bitcast.116, f32[8,512,128,4]{2,1,3,0:T(8,128)} %fusion.39, f32[8,512,128,4]{2,1,3,0:T(8,128)} %copy-done, f32[8,4,128]{2,1,0:T(4,128)S(1)} %bitcast.137, pred[128,512]{0,1:T(8,128)(4,1)S(1)} %compare_and_fusion), kind=kOutput, calls=%fused_computation.17 | convolution fusion | flops 564662784 | bytes 18956288 | tf_op jit(solution)/shard_map/agtk,kad->tagd/dot_general | solution.py:65
  259.3 1.3 copy.91
  (26 shorter events, 4.5 us)
Async XLA Ops:
  7.2 62.8 %all-gather.5.cloned.1.call-start = ((), (), s32[]{:S(2)}) async-start(), calls=%async_computation.8 | async-start | bytes 1114112 | tf_op jit(solution)/shard_map/all_gather | solution.py:43
  34.5 12.7 %all-to-all-start.1 = ((bf16[32,2,512]{2,1,0:T(2,128)(2,1)}), bf16[32,2,512]{2,1,0:T(2,128)(2,1)S(1)}, u32[]{:S(2)}, u32[]{:S(2)}) async-start(bf16[32,2,512]{2,1,0:T(2,128)(2,1)} %reshape.119), calls=%async_computation.1 | async-start | bytes 131072 | tf_op jit(solution)/shard_map/all_to_all | solution.py:38
  38.4 74.2 %all-gather.7.cloned.1.call-start = ((), (), s32[]{:S(2)}) async-start(), calls=%async_computation.9 | async-start | bytes 1114112 | tf_op jit(solution)/shard_map/all_gather | solution.py:44
  48.0 124.2 %reduce-scatter.5.cloned.1.call-start = ((), (), s32[]{:S(2)}) async-start(), calls=%async_computation.7 | async-start | bytes 1114112 | tf_op jit(solution)/shard_map/reduce_scatter | solution.py:81
  72.9 5.3 %copy-start = (f32[8,512,128,4]{2,1,3,0:T(8,128)}, f32[8,512,128,4]{2,1,3,0:T(8,128)S(1)}, u32[]{:S(2)}) copy-start(f32[8,512,128,4]{2,1,3,0:T(8,128)S(1)} %get-tuple-element.19) | copy-start | bytes 25165828
  80.5 154.1 %reduce-scatter.3.cloned.1.call-start = ((), (), s32[]{:S(2)}) async-start(), calls=%async_computation.6 | async-start | bytes 1114112 | tf_op jit(solution)/shard_map/reduce_scatter | solution.py:78
  174.7 62.5 %all-to-all-start.3 = ((bf16[32,2,512]{2,1,0:T(2,128)(2,1)}), bf16[32,2,512]{2,1,0:T(2,128)(2,1)S(1)}, u32[]{:S(2)}, u32[]{:S(2)}) async-start(bf16[32,2,512]{2,1,0:T(2,128)(2,1)} %reshape.123), calls=%async_computation.5 | async-start | bytes 131072 | tf_op jit(solution)/shard_map/all_to_all | solution.py:89
  237.2 24.1 %all-to-all-start.2 = ((bf16[32,2,512]{2,1,0:T(2,128)(2,1)}), bf16[32,2,512]{2,1,0:T(2,128)(2,1)S(1)}, u32[]{:S(2)}, u32[]{:S(2)}) async-start(bf16[32,2,512]{2,1,0:T(2,128)(2,1)} %reshape.121), calls=%async_computation.3 | async-start | bytes 131072 | tf_op jit(solution)/shard_map/all_to_all | solution.py:86
Sparse Core Ops, SparseCore 0:
  32.5 37.4 all-gather.4
  72.7 39.8 all-gather.6
  115.4 56.6 reduce-scatter.4
  175.6 58.9 reduce-scatter.2
where the time goes:
time: 272 us; the launch traced here: 269 us
  waiting for transfers between devices  145 us (53%)
  matrix products  37.5 us (14%)
  blocking collectives  22.3 us (8%)
  starting transfers between devices  21.5 us (8%)
  local copies, waits for them, and re-layouts  19.2 us (7%)
  between operations  13.9 us (5%)
  other arithmetic  8.65 us (3%)
    reduce_scatter x1, waiting for transfers between devices, shards(): lax.psum_scatter(grad_key_all.astype(jnp.bfloat16), 'ctx', scatter_dimens...  51.1 us
    reduce_scatter x1, waiting for transfers between devices, shards(): lax.psum_scatter(grad_value_all.astype(jnp.bfloat16), 'ctx', scatter_dime...  36.5 us
    all_gather x1, waiting for transfers between devices, shards(): lax.all_gather(own_values, 'ctx', axis=0, tiled=True)  31.9 us
    all_to_all x1, blocking collectives, shards(): lax.all_to_all(img_k, 'enc', split_axis=0, concat_axis=1, tiled=True)  22.3 us
    all_gather x1, waiting for transfers between devices, shards(): lax.all_gather(own_keys, 'ctx', axis=0, tiled=True)  22 us
    dot_general x1, matrix products, shards(): jnp.einsum('agtk,tagd->kad', grad_scores, query_heads, preferred_element_...  13.7 us
    dot_general x1, matrix products, shards(): jnp.einsum('agtk,kad->tagd', grad_scores, key_heads, preferred_element_ty...  13.5 us
    all_to_all x1, starting transfers between devices, shards(): lax.all_to_all(value_sums.astype(jnp.bfloat16)[None], 'enc', split_axis=1...  8.77 us
  transfers between devices with their start and end apart: 7, of which 5 were waited for; matrix products, arithmetic and copies ran while one was open for 23% of the time, Pallas kernels for 0%

commit v1 on v0

v1 whole, which is shorter than its diff:
```python
import functools
import math

import jax
import jax.numpy as jnp
from jax import lax
from jax.experimental import pallas as pl
from jax.experimental.pallas import tpu as pltpu
from jax.sharding import PartitionSpec as P

H = 32
KVH = 8
HD = 128
SAMP = 2
MAX_TILES = 4
RING = SAMP * MAX_TILES
HALF_KV = KVH // 2
RATIO = H // KVH
SCALE = HD ** -0.5
EXP2_SCALE = SCALE * math.log2(math.e)

big_negative = -1e30

MESH = pl.DeviceIdType.MESH
F32 = jnp.float32
BF16 = jnp.bfloat16


def remote(src, dst, send_sem, recv_sem, ctx, enc):
    return pltpu.make_async_remote_copy(
        src_ref=src,
        dst_ref=dst,
        send_sem=send_sem,
        recv_sem=recv_sem,
        device_id=(ctx, enc),
        device_id_type=MESH,
    )


def nt_dot(a, b):
    return lax.dot_general(a, b, (((1,), (1,)), ((), ())), preferred_element_type=F32)


def kernel(
    n_enc,
    tiles_ref,
    text_ref,
    own_ref,
    q_ref,
    do_ref,
    dq_ref,
    dkv_ref,
    text_buf,
    late_mask,
    q_buf,
    do_buf,
    dq_buf,
    slots,
    rows,
    kv,
    ds_all,
    p_all,
    qc_all,
    dc_all,
    part,
    rs_send,
    rs_recv,
    load_sem,
    swap_send,
    swap_recv,
    in_send,
    in_recv,
    ag_send,
    ag_recv,
    red_send,
    red_recv,
    out_send,
    out_recv,
    dq_sem,
    dq_send,
    dq_recv,
):
    ctx = lax.axis_index("ctx")
    enc = lax.axis_index("enc")
    y = ctx // 2
    core = lax.rem(ctx, 2)
    other = 1 - core
    twin = 2 * y + other
    right = 2 * lax.rem(y + 1, RING) + core
    left = 2 * lax.rem(y + RING - 1, RING) + core
    tokens = q_ref.shape[0]
    width = q_ref.shape[1] // 2
    tile = 2 * n_enc
    span = MAX_TILES * tile

    mine = pl.ds(pl.multiple_of(core * width, width), width)
    theirs = pl.ds(pl.multiple_of(other * width, width), width)

    load_q = pltpu.make_async_copy(q_ref.at[:, mine], q_buf.at[core], load_sem.at[0])
    load_do = pltpu.make_async_copy(do_ref.at[:, mine], do_buf.at[core], load_sem.at[1])
    load_q.start()
    load_do.start()

    barrier = pltpu.get_barrier_semaphore()
    pl.semaphore_signal(barrier, inc=1, device_id=(right, enc), device_id_type=MESH)
    pl.semaphore_signal(barrier, inc=1, device_id=(left, enc), device_id_type=MESH)
    pl.semaphore_signal(barrier, inc=1, device_id=(twin, enc), device_id_type=MESH)

    def greet(i, carry):
        peer = lax.rem(enc + i, n_enc)
        pl.semaphore_signal(barrier, inc=1, device_id=(2 * y, peer), device_id_type=MESH)
        pl.semaphore_signal(barrier, inc=1, device_id=(2 * y + 1, peer), device_id_type=MESH)
        return carry

    lax.fori_loop(1, n_enc, greet, 0)
    pl.semaphore_wait(barrier, 2 * n_enc + 1)

    here = core * n_enc + enc
    keep_in = pltpu.make_async_copy(own_ref.at[enc, core], slots.at[here], in_recv)
    keep_in.start()
    remote(own_ref.at[enc, other], slots.at[here], in_send, in_recv, twin, enc).start()

    def scatter_in(i, carry):
        peer = lax.rem(enc + i, n_enc)
        remote(own_ref.at[peer, 0], slots.at[here], in_send, in_recv, 2 * y, peer).start()
        remote(own_ref.at[peer, 1], slots.at[here], in_send, in_recv, 2 * y + 1, peer).start()
        return carry

    lax.fori_loop(1, n_enc, scatter_in, 0)

    swaps = [
        remote(text_ref, text_buf.at[core], swap_send.at[0], swap_recv.at[0], twin, enc),
        remote(q_ref.at[:, theirs], q_buf.at[core], swap_send.at[1], swap_recv.at[1], twin, enc),
        remote(do_ref.at[:, theirs], do_buf.at[core], swap_send.at[2], swap_recv.at[2], twin, enc),
    ]
    for swap in swaps:
        swap.start()

    pltpu.make_async_copy(slots, slots, in_recv).wait()
    rows[...] = slots[...].astype(F32).reshape(rows.shape)
    for kind in range(2):
        for a in range(HALF_KV):
            lines = rows[pl.ds(kind * HALF_KV + a, tile, stride=2 * HALF_KV), :]
            kv[y, a, kind] = lines.astype(BF16)

    def ag_copy(way, hop, a, block):
        target = right if way == 0 else left
        return remote(
            kv.at[block, a],
            kv.at[block, a],
            ag_send.at[way, hop - 1, a],
            ag_recv.at[way, hop - 1, a],
            target,
            enc,
        )

    def ag_first(a, carry):
        ag_copy(0, 1, a, y).start()
        ag_copy(1, 1, a, y).start()
        return carry

    lax.fori_loop(0, HALF_KV, ag_first, 0)

    text_buf[core] = text_ref[...]
    swaps[0].wait_recv()
    text_row = jnp.concatenate([text_buf[0], text_buf[1]], axis=1)
    for half in range(2):
        spread = jnp.broadcast_to(text_buf[half].astype(F32), (HD, tokens))
        late_mask[half * tokens:(half + 1) * tokens, :] = spread.T.astype(BF16)
    limit = jnp.where(text_row == 0, tiles_ref[0, 0], tiles_ref[0, 1])
    biases = [jnp.where(limit > t, 0.0, big_negative).astype(F32) for t in range(MAX_TILES)]
    early = text_row == 0

    for hop in range(1, 4):
        behind = lax.rem(y + RING - hop, RING)
        ahead = lax.rem(y + hop, RING)

        def ag_step(a, carry, hop=hop, behind=behind, ahead=ahead):
            ag_copy(0, hop, a, behind).wait_recv()
            ag_copy(1, hop, a, ahead).wait_recv()
            if hop < 3:
                ag_copy(0, hop + 1, a, behind).start()
                ag_copy(1, hop + 1, a, ahead).start()
            return carry

        lax.fori_loop(0, HALF_KV, ag_step, 0)
        if hop == 3:
            for a in range(2):
                ag_copy(0, 4, a, behind).start()
                ag_copy(1, 4, a + 2, ahead).start()

    load_q.wait()
    load_do.wait()
    swaps[1].wait_recv()
    swaps[2].wait_recv()

    far = lax.rem(y + 4, RING)

    def rs_copy(way, hop, a):
        target = right if way == 0 else left
        return remote(
            rs_send.at[way, hop - 1, a],
            rs_recv.at[way, hop - 1, a],
            red_send.at[way, hop - 1, a],
            red_recv.at[way, hop - 1, a],
            target,
            enc,
        )

    def head(a, carry):
        remote(
            kv.at[far, a], kv.at[far, a], ag_send.at[a // 2, 3, a], ag_recv.at[a // 2, 3, a], right, enc
        ).wait_recv()
        keys = jnp.concatenate(
            [kv[0:MAX_TILES, a, 0].reshape(span, HD), kv[MAX_TILES:RING, a, 0].reshape(span, HD)], axis=1
        )
        values = jnp.concatenate(
            [kv[0:MAX_TILES, a, 1].reshape(span, HD), kv[MAX_TILES:RING, a, 1].reshape(span, HD)], axis=1
        )
        keys_t = keys.T
        late = late_mask[...]
        for r in range(RATIO):
            cols = pl.ds(pl.multiple_of((a * RATIO + r) * HD, HD), HD)
            block = slice(r * 2 * tokens, (r + 1) * 2 * tokens)
            q = q_buf[:, :, cols].reshape(2 * tokens, HD)
            q_late = q * late
            qc = jnp.concatenate([q - q_late, q_late], axis=1)
            d = do_buf[:, :, cols].reshape(2 * tokens, HD)
            d_late = d * late
            dc = jnp.concatenate([d - d_late, d_late], axis=1)
            qc_all[block, :] = qc
            dc_all[block, :] = dc
            s = nt_dot(keys, qc)
            g = nt_dot(values, dc)
            s = jnp.concatenate(
                [s[t * tile:(t + 1) * tile] + biases[t] for t in range(MAX_TILES)], axis=0
            )
            top = jnp.max(s, axis=0, keepdims=True)
            e = jnp.exp2((s - top) * EXP2_SCALE)
            inv = 1.0 / jnp.sum(e, axis=0, keepdims=True)
            row_dot = jnp.sum(e * g, axis=0, keepdims=True) * inv
            p_all[:, block] = (e * inv).astype(BF16)
            ds = (e * ((g - row_dot) * (inv * SCALE))).astype(BF16)
            ds_all[:, block] = ds
            both = jnp.dot(keys_t, ds, preferred_element_type=F32)
            dq = jnp.where(early, both[:HD], both[HD:]).T.astype(BF16)
            dq_buf[:, :, cols] = dq.reshape(2, tokens, HD)
        dk = jnp.dot(ds_all[...], qc_all[...], preferred_element_type=F32)
        dv = jnp.dot(p_all[...], dc_all[...], preferred_element_type=F32)
        for sample in range(SAMP):
            for t in range(MAX_TILES):
                window = (slice(t * tile, (t + 1) * tile), slice(sample * HD, (sample + 1) * HD))
                part[a, sample * MAX_TILES + t, 0] = dk[window]
                part[a, sample * MAX_TILES + t, 1] = dv[window]
        hop_r = 4 - a // 2
        hop_l = 3 + a // 2
        rs_send[0, hop_r - 1, a] = part[a, lax.rem(y + hop_r, RING)].astype(BF16)
        rs_copy(0, hop_r, a).start()
        rs_send[1, hop_l - 1, a] = part[a, lax.rem(y + RING - hop_l, RING)].astype(BF16)
        rs_copy(1, hop_l, a).start()
        return carry

    lax.fori_loop(0, HALF_KV, head, 0)

    dq_keep = pltpu.make_async_copy(dq_buf.at[core], dq_ref.at[:, mine], dq_sem)
    dq_keep.start()
    dq_swap = remote(dq_buf.at[other], dq_ref.at[:, mine], dq_send, dq_recv, twin, enc)
    dq_swap.start()

    def rs_add(way, hop, a):
        rs_copy(way, hop + 1, a).wait_recv()
        dest = lax.rem(y + hop, RING) if way == 0 else lax.rem(y + RING - hop, RING)
        total = part[a, dest] + rs_recv[way, hop, a].astype(F32)
        rs_send[way, hop - 1, a] = total.astype(BF16)
        rs_copy(way, hop, a).start()

    for a in range(2):
        rs_add(0, 3, a)
        rs_add(1, 3, a + 2)
    for hop in (2, 1):

        def rs_step(a, carry, hop=hop):
            rs_add(0, hop, a)
            rs_add(1, hop, a)
            return carry

        lax.fori_loop(0, HALF_KV, rs_step, 0)

    for a in range(HALF_KV):
        rs_copy(0, 1, a).wait_recv()
        rs_copy(1, 1, a).wait_recv()
        total = part[a, y] + rs_recv[0, 0, a].astype(F32) + rs_recv[1, 0, a].astype(F32)
        for kind in range(2):
            rows[pl.ds(kind * HALF_KV + a, tile, stride=2 * HALF_KV), :] = total[kind]

    pltpu.make_async_copy(slots.at[pl.ds(0, tile - 1)], slots.at[pl.ds(0, tile - 1)], in_send).wait()
    slots[...] = rows[...].reshape(slots.shape).astype(BF16)
    keep_out = pltpu.make_async_copy(slots.at[here], dkv_ref.at[enc, core], out_recv)
    keep_out.start()
    remote(
        slots.at[other * n_enc + enc], dkv_ref.at[enc, core], out_send, out_recv, twin, enc
    ).start()

    def scatter_out(i, carry):
        peer = lax.rem(enc + i, n_enc)
        remote(slots.at[peer], dkv_ref.at[enc, core], out_send, out_recv, 2 * y, peer).start()
        remote(slots.at[n_enc + peer], dkv_ref.at[enc, core], out_send, out_recv, 2 * y + 1, peer).start()
        return carry

    lax.fori_loop(1, n_enc, scatter_out, 0)

    for swap in swaps:
        swap.wait_send()

    def drain(a, carry):
        for way in range(2):
            for hop in range(1, 4):
                ag_copy(way, hop, a, y).wait_send()
                rs_copy(way, hop, a).wait_send()
        remote(
            kv.at[far, a], kv.at[far, a], ag_send.at[a // 2, 3, a], ag_recv.at[a // 2, 3, a], right, enc
        ).wait_send()
        remote(
            rs_send.at[a // 2, 3, a],
            rs_recv.at[a // 2, 3, a],
            red_send.at[a // 2, 3, a],
            red_recv.at[a // 2, 3, a],
            right,
            enc,
        ).wait_send()
        return carry

    lax.fori_loop(0, HALF_KV, drain, 0)
    dq_keep.wait()
    dq_swap.wait()
    pltpu.make_async_copy(slots.at[pl.ds(0, tile - 1)], slots.at[pl.ds(0, tile - 1)], out_send).wait()
    pltpu.make_async_copy(dkv_ref, dkv_ref, out_recv).wait()


def shards(n_enc, queries, d_out, text_sample, tiles, img_k, img_v):
    tokens, width = queries.shape[1:]
    tile = 2 * n_enc
    span = MAX_TILES * tile
    rows = HALF_KV * 2
    own = jnp.concatenate(
        [img_k.reshape(n_enc, 2, HALF_KV, HD), img_v.reshape(n_enc, 2, HALF_KV, HD)], axis=2
    )
    vmem = pl.BlockSpec(memory_space=pltpu.VMEM)
    anywhere = pl.BlockSpec(memory_space=pl.ANY)
    dma = pltpu.SemaphoreType.DMA
    d_queries, d_own = pl.pallas_call(
        functools.partial(kernel, n_enc),
        out_shape=(
            jax.ShapeDtypeStruct((tokens, width), BF16),
            jax.ShapeDtypeStruct((n_enc, 2, rows, HD), BF16),
        ),
        in_specs=[pl.BlockSpec(memory_space=pltpu.SMEM), vmem, anywhere, anywhere, anywhere],
        out_specs=(anywhere, anywhere),
        scratch_shapes=[
            pltpu.VMEM((2, 1, tokens), jnp.int32),
            pltpu.VMEM((2 * tokens, HD), BF16),
            pltpu.VMEM((2, tokens, width // 2), BF16),
            pltpu.VMEM((2, tokens, width // 2), BF16),
            pltpu.VMEM((2, tokens, width // 2), BF16),
            pltpu.VMEM((tile, rows, HD), BF16),
            pltpu.VMEM((tile * rows, HD), F32),
            pltpu.VMEM((RING, HALF_KV, 2, tile, HD), BF16),
            pltpu.VMEM((span, RATIO * 2 * tokens), BF16),
            pltpu.VMEM((span, RATIO * 2 * tokens), BF16),
            pltpu.VMEM((RATIO * 2 * tokens, 2 * HD), BF16),
            pltpu.VMEM((RATIO * 2 * tokens, 2 * HD), BF16),
            pltpu.VMEM((HALF_KV, RING, 2, tile, HD), F32),
            pltpu.VMEM((2, 4, HALF_KV, 2, tile, HD), BF16),
            pltpu.VMEM((2, 4, HALF_KV, 2, tile, HD), BF16),
            dma((2,)),
            dma((3,)),
            dma((3,)),
            dma,
            dma,
            dma((2, 4, HALF_KV)),
            dma((2, 4, HALF_KV)),
            dma((2, 4, HALF_KV)),
            dma((2, 4, HALF_KV)),
            dma,
            dma,
            dma,
            dma,
            dma,
        ],
        compiler_params=pltpu.CompilerParams(
            collective_id=0, has_side_effects=True, vmem_limit_bytes=40 * 1024 * 1024
        ),
    )(tiles, text_sample, own, queries[0], d_out[0])
    back_keys = d_own[:, :, :HALF_KV].reshape(n_enc, 1, KVH * HD)
    back_values = d_own[:, :, HALF_KV:].reshape(n_enc, 1, KVH * HD)
    return (d_queries[None], back_keys, back_values)


def solution(mesh):
    in_specs = (
        P("enc", "ctx", None),
        P("enc", "ctx", None),
        P("enc", "ctx"),
        P("enc", None),
        P(None, ("ctx", "enc"), None),
        P(None, ("ctx", "enc"), None),
    )
    out_specs = (
        P("enc", "ctx", None),
        P(None, ("ctx", "enc"), None),
        P(None, ("ctx", "enc"), None),
    )
    return jax.shard_map(
        functools.partial(shards, mesh.shape["enc"]),
        mesh=mesh,
        in_specs=in_specs,
        out_specs=out_specs,
        check_vma=False,
    )
```

time: 272 us -> 76.5 us (0.28); the launches traced: 269 us -> 76.2 us
  waiting for transfers between devices: 145 us -> 0 us
  Pallas kernels: 0 us -> 69.2 us
  matrix products: 37.5 us -> 0 us
  blocking collectives: 22.3 us -> 0 us
  starting transfers between devices: 21.5 us -> 0 us
  between operations: 13.9 us -> 0.7 us
  local copies, waits for them, and re-layouts: 19.2 us -> 6.3 us
  other arithmetic: 8.65 us -> 0.07 us
    reduce_scatter x2 -> x0, waiting for transfers between devices: 87.6 us -> none  [the longest x1 51.1 us: shards(): lax.psum_scatter(grad_key_all.astype(jnp.bfloat16), 'ctx', scatter_dimens...]
    pallas_call x0 -> x1, Pallas kernels: none -> 69.2 us  [shards(): pl.pallas_call(functools.partial(kernel, n_enc), out_shape=(jax.ShapeDtyp...]
    all_gather x2 -> x0, waiting for transfers between devices: 53.9 us -> none  [the longest x1 31.9 us: shards(): lax.all_gather(own_values, 'ctx', axis=0, tiled=True)]
    dot_general x5 -> x0, matrix products: 37.5 us -> none  [the longest x1 13.7 us: shards(): jnp.einsum('agtk,tagd->kad', grad_scores, query_heads, preferred_element_...]
    all_to_all x1 -> x0, blocking collectives: 22.3 us -> none  [shards(): lax.all_to_all(img_k, 'enc', split_axis=0, concat_axis=1, tiled=True)]
    all_to_all x3 -> x0, starting transfers between devices: 21.2 us -> none  [the longest x1 8.77 us: shards(): lax.all_to_all(value_sums.astype(jnp.bfloat16)[None], 'enc', split_axis=1...]
    unnamed x4 -> x0, other arithmetic: 4.95 us -> none
    all_to_all x3 -> x0, waiting for transfers between devices: 3.96 us -> none  [the longest x1 3.96 us: shards(): lax.all_to_all(img_v, 'enc', split_axis=0, concat_axis=1, tiled=True)]
  transfers between devices with their start and end apart: 7 -> 0, of which waited for: 5 -> 0; matrix products, arithmetic and copies ran while one was open for 23% -> 0% of each run, Pallas kernels for 0% -> 0%
where the time goes in v1:
time: 76.5 us; the launch traced here: 76.2 us
  Pallas kernels  69.2 us (90%)
  local copies, waits for them, and re-layouts  6.3 us (8%)
    pallas_call x1, Pallas kernels, shards(): pl.pallas_call(functools.partial(kernel, n_enc), out_shape=(jax.ShapeDtyp...  69.2 us
    unnamed x11, local copies, waits for them, and re-layouts  4 us

profile of v1, /device:TPU:1, one launch (start us, length us, event | category | flops | bytes accessed | tf_op | source)
XLA Modules:
  0.0 76.2 jit_solution(6816216598999561770)
XLA Ops:
  0.6 0.0 copy-start.4
  0.6 0.9 %reshape.18 = bf16[32,2,4,128]{3,2,1,0:T(4,128)(2,1)S(1)} reshape(bf16[32,1,1024]{2,0,1:T(8,128)(2,1)} %param.10) | data formatting | bytes 131072 | tf_op jit(solution)/shard_map/reshape | solution.py:346
  1.5 0.0 copy-done.4
  1.6 0.0 copy-start.2
  1.6 0.0 copy-start.3
  1.6 0.1 pad_maximum_fusion.own_ref
  1.7 0.6 copy-done.2
  2.3 0.0 copy-done.3
  2.3 0.0 copy-start
  2.3 1.2 %copy-done = bf16[1,128,4096]{2,1,0:T(8,128)(2,1)S(1)} copy-done((bf16[1,128,4096]{2,1,0:T(8,128)(2,1)S(1)}, bf16[1,128,4096]{2,1,0:T(8,128)(2,1)}, u32[]{:S(2)}) %copy-start) | copy-done | bytes 1048600
  3.5 0.0 copy-start.1
  3.5 1.2 %copy-done.1 = bf16[1,128,4096]{2,1,0:T(8,128)(2,1)S(1)} copy-done((bf16[1,128,4096]{2,1,0:T(8,128)(2,1)S(1)}, bf16[1,128,4096]{2,1,0:T(8,128)(2,1)}, u32[]{:S(2)}) %copy-start.1) | copy-done | bytes 1048600
  4.7 69.2 %shard_map.85 = (bf16[128,4096]{1,0:T(8,128)(2,1)S(1)}, bf16[32,2,8,128]{3,2,1,0:T(8,128)(2,1)S(1)}) custom-call(s32[1,2]{1,0:T(1,128)S(1)} %copy-done.2, s32[1,128]{1,0:T(1,128)S(1)} %copy-done.3, bf16[32,2,8,128]{3,2,1,0:T(8,128)(2,1)S(1)} %pad_maximum_fusion.own_ref, bf16[128,4096]{1,0:T(8,128)(2,1)S(1)} %bitcast.7, bf16[128,4096]{1,0:T(8,128)(2,1)S(1)} %bitcast.8), custom_call_target="tpu_custom_call" | custom-call | tf_op jit(solution)/shard_map/pallas_call | solution.py:351
  74.0 0.7 reshape.21
  74.6 0.7 reshape.20
  75.3 1.0 %copy.10 = bf16[1,128,4096]{2,1,0:T(8,128)(2,1)} copy(bf16[1,128,4096]{2,1,0:T(8,128)(2,1)S(1)} %bitcast.9) | data formatting | bytes 2097152
  (2 shorter events, 0.1 us)
Async XLA Ops:
  0.6 0.9 %copy-start.4 = (bf16[32,1,1024]{2,0,1:T(8,128)(2,1)S(1)}, bf16[32,1,1024]{2,0,1:T(8,128)(2,1)}, u32[]{:S(2)}) copy-start(bf16[32,1,1024]{2,0,1:T(8,128)(2,1)} %param.11) | copy-start | bytes 196612
  1.6 0.7 copy-start.2
  1.6 0.7 copy-start.3
  2.3 1.2 %copy-start = (bf16[1,128,4096]{2,1,0:T(8,128)(2,1)S(1)}, bf16[1,128,4096]{2,1,0:T(8,128)(2,1)}, u32[]{:S(2)}) copy-start(bf16[1,128,4096]{2,1,0:T(8,128)(2,1)} %param.6) | copy-start | bytes 3145732
  3.5 1.2 %copy-start.1 = (bf16[1,128,4096]{2,1,0:T(8,128)(2,1)S(1)}, bf16[1,128,4096]{2,1,0:T(8,128)(2,1)}, u32[]{:S(2)}) copy-start(bf16[1,128,4096]{2,1,0:T(8,128)(2,1)} %param.7) | copy-start | bytes 3145732

commit v2 on v1

v2 whole, which is shorter than its diff:
```python
import functools
import math

import jax
import jax.numpy as jnp
from jax import lax
from jax.experimental import pallas as pl
from jax.experimental.pallas import tpu as pltpu
from jax.sharding import PartitionSpec as P

H = 32
KVH = 8
HD = 128
SAMP = 2
MAX_TILES = 4
RING = SAMP * MAX_TILES
HALF_KV = KVH // 2
RATIO = H // KVH
SCALE = HD ** -0.5
EXP2_SCALE = SCALE * math.log2(math.e)

big_negative = -1e30
VMEM_LIMIT = 58 * 1024 * 1024

MESH = pl.DeviceIdType.MESH
F32 = jnp.float32
BF16 = jnp.bfloat16


def remote(src, dst, send_sem, recv_sem, ctx, enc):
    return pltpu.make_async_remote_copy(
        src_ref=src,
        dst_ref=dst,
        send_sem=send_sem,
        recv_sem=recv_sem,
        device_id=(ctx, enc),
        device_id_type=MESH,
    )


def peer_of(n_enc, enc, i):
    if n_enc != 32:
        return lax.rem(enc + i + 1, n_enc)
    far_z = i // 4
    near = (far_z + 1) // 2
    z = lax.rem(enc // 4 + 12 + near - 2 * near * lax.rem(far_z + 1, 2), 8)
    far_x = lax.rem(i, 4)
    x = lax.rem(enc + 2 + far_x + far_x // 2 * (1 - 2 * lax.rem(far_x, 2)), 4)
    return 4 * z + x


def nt_dot(a, b):
    return lax.dot_general(a, b, (((1,), (1,)), ((), ())), preferred_element_type=F32)


def kernel(
    n_enc,
    tiles_hbm,
    text_hbm,
    k_ref,
    v_ref,
    q_ref,
    do_ref,
    dq_ref,
    dkv_ref,
    tiles_ref,
    text_buf,
    kv_in,
    own_ref,
    late_mask,
    q_buf,
    do_buf,
    dq_buf,
    slots,
    rows,
    kv,
    ds_all,
    p_all,
    qc_all,
    dc_all,
    part,
    rs_send,
    rs_recv,
    load_sem,
    swap_send,
    swap_recv,
    in_send,
    in_recv,
    ag_send,
    ag_recv,
    red_send,
    red_recv,
    out_send,
    out_recv,
    dq_sem,
    dq_send,
    dq_recv,
    small_sem,
):
    ctx = lax.axis_index("ctx")
    enc = lax.axis_index("enc")
    y = ctx // 2
    core = lax.rem(ctx, 2)
    other = 1 - core
    twin = 2 * y + other
    ahead = [2 * lax.rem(y + step, RING) + core for step in (1, 2)]
    behind = [2 * lax.rem(y + RING - step, RING) + core for step in (1, 2)]
    along = [ahead, behind]
    tokens = q_ref.shape[0]
    width = q_ref.shape[1] // 2
    tile = 2 * n_enc
    span = MAX_TILES * tile

    mine = pl.ds(pl.multiple_of(core * width, width), width)
    theirs = pl.ds(pl.multiple_of(other * width, width), width)

    barrier = pltpu.get_barrier_semaphore()
    pl.semaphore_signal(barrier, inc=1, device_id=(twin, enc), device_id_type=MESH)
    for step in range(2):
        pl.semaphore_signal(barrier, inc=1, device_id=(ahead[step], enc), device_id_type=MESH)
        pl.semaphore_signal(barrier, inc=1, device_id=(behind[step], enc), device_id_type=MESH)

    def greet(i, carry):
        peer = peer_of(n_enc, enc, i)
        pl.semaphore_signal(barrier, inc=1, device_id=(2 * y, peer), device_id_type=MESH)
        pl.semaphore_signal(barrier, inc=1, device_id=(2 * y + 1, peer), device_id_type=MESH)
        return carry

    lax.fori_loop(0, n_enc - 1, greet, 0)
    load_k = pltpu.make_async_copy(k_ref, kv_in.at[0], small_sem.at[0])
    load_v = pltpu.make_async_copy(v_ref, kv_in.at[1], small_sem.at[1])
    load_tiles = pltpu.make_async_copy(tiles_hbm, tiles_ref, small_sem.at[2])
    load_text = pltpu.make_async_copy(text_hbm, text_buf.at[core], small_sem.at[3])
    load_q = pltpu.make_async_copy(q_ref.at[:, mine], q_buf.at[core], load_sem.at[0])
    load_do = pltpu.make_async_copy(do_ref.at[:, mine], do_buf.at[core], load_sem.at[1])
    loads = [load_k, load_v, load_tiles, load_text, load_q, load_do]
    for load in loads:
        load.start()

    load_k.wait()
    load_v.wait()
    for kind in range(2):
        for h in range(KVH):
            first = h // HALF_KV * 2 * HALF_KV + kind * HALF_KV + h % HALF_KV
            piece = kv_in[kind, :, h * HD:(h + 1) * HD]
            rows[pl.ds(first, n_enc, stride=4 * HALF_KV), :] = piece.astype(F32)
    own_ref[...] = rows[...].reshape(own_ref.shape).astype(BF16)

    pl.semaphore_wait(barrier, 2 * n_enc + 3)

    here = core * n_enc + enc
    def scatter_in(i, carry):
        peer = peer_of(n_enc, enc, i)
        remote(own_ref.at[peer, 0], slots.at[here], in_send, in_recv, 2 * y, peer).start()
        remote(own_ref.at[peer, 1], slots.at[here], in_send, in_recv, 2 * y + 1, peer).start()
        return carry

    lax.fori_loop(0, n_enc - 1, scatter_in, 0)

    keep_in = pltpu.make_async_copy(own_ref.at[enc, core], slots.at[here], in_recv)
    keep_in.start()
    remote(own_ref.at[enc, other], slots.at[here], in_send, in_recv, twin, enc).start()

    swaps = [
        remote(text_hbm, text_buf.at[core], swap_send.at[0], swap_recv.at[0], twin, enc),
        remote(q_ref.at[:, theirs], q_buf.at[core], swap_send.at[1], swap_recv.at[1], twin, enc),
        remote(do_ref.at[:, theirs], do_buf.at[core], swap_send.at[2], swap_recv.at[2], twin, enc),
    ]
    for swap in swaps:
        swap.start()

    pltpu.make_async_copy(slots, slots, in_recv).wait()
    rows[...] = slots[...].astype(F32).reshape(rows.shape)
    for kind in range(2):
        for a in range(HALF_KV):
            lines = rows[pl.ds(kind * HALF_KV + a, tile, stride=2 * HALF_KV), :]
            kv[y, a, kind] = lines.astype(BF16)

    def ag_copy(way, a, offset, step):
        block = lax.rem(y + RING - offset, RING) if way == 0 else lax.rem(y + offset, RING)
        sem = offset + step - 1
        return remote(
            kv.at[block, a], kv.at[block, a], ag_send.at[way, sem, a], ag_recv.at[way, sem, a], along[way][step - 1], enc
        )

    def ag_wait(way, a, offset):
        block = lax.rem(y + RING - offset, RING) if way == 0 else lax.rem(y + offset, RING)
        sem = offset - 1
        remote(
            kv.at[block, a], kv.at[block, a], ag_send.at[way, sem, a], ag_recv.at[way, sem, a], along[way][0], enc
        ).wait_recv()

    for step in (2, 1):

        def ag_first(a, carry, step=step):
            ag_copy(0, a, 0, step).start()
            ag_copy(1, a, 0, step).start()
            return carry

        lax.fori_loop(0, HALF_KV, ag_first, 0)

    load_tiles.wait()
    load_text.wait()
    swaps[0].wait_recv()
    text_row = jnp.concatenate([text_buf[0], text_buf[1]], axis=1)
    for half in range(2):
        spread = jnp.broadcast_to(text_buf[half].astype(F32), (HD, tokens))
        late_mask[half * tokens:(half + 1) * tokens, :] = spread.T.astype(BF16)
    limit = jnp.where(text_row == 0, tiles_ref[0, 0], tiles_ref[0, 1])
    biases = [jnp.where(limit > t, 0.0, big_negative).astype(F32) for t in range(MAX_TILES)]
    early = text_row == 0

    for a in range(HALF_KV):
        for way in range(2):
            ag_wait(way, a, 2)
            if way == a // 2:
                ag_copy(way, a, 2, 2).start()
            ag_copy(way, a, 2, 1).start()

    load_q.wait()
    load_do.wait()
    swaps[1].wait_recv()
    swaps[2].wait_recv()

    far = lax.rem(y + 4, RING)

    def far_copy(a):
        side = a // 2
        return remote(
            kv.at[far, a], kv.at[far, a], ag_send.at[side, 3, a], ag_recv.at[side, 3, a], along[0][0], enc
        )

    def rs_copy(way, kind, a, target):
        return remote(
            rs_send.at[way, kind, a],
            rs_recv.at[way, kind, a],
            red_send.at[way, kind, a],
            red_recv.at[way, kind, a],
            target,
            enc,
        )

    def due(way, steps):
        return lax.rem(y + steps, RING) if way == 0 else lax.rem(y + RING - steps, RING)

    def rs_first(a):
        side = a // 2
        rs_send[side, 1, a] = part[a, far].astype(BF16)
        rs_copy(side, 1, a, ahead[1] + side * (behind[1] - ahead[1])).start()
        for way in range(2):
            rs_send[way, 0, a] = part[a, due(way, 3)].astype(BF16)
            rs_copy(way, 0, a, along[way][0]).start()
        for way in range(2):
            rs_send[way, 2, a] = part[a, due(way, 1)].astype(BF16)
            rs_copy(way, 2, a, along[way][0]).start()

    def rs_second(a, side):
        for way in range(2):
            total = part[a, due(way, 2)]
            rs_copy(way, 0, a, along[way][0]).wait_recv()
            total = total + rs_recv[way, 0, a].astype(F32)
            if way == side:
                rs_copy(way, 1, a, along[way][0]).wait_recv()
                total = total + rs_recv[way, 1, a].astype(F32)
            rs_send[way, 3, a] = total.astype(BF16)
            rs_copy(way, 3, a, along[way][1]).start()

    def head(a, carry):
        for way in range(2):
            ag_wait(way, a, 1)
            ag_wait(way, a, 3)
        far_copy(a).wait_recv()
        keys = jnp.concatenate(
            [kv[0:MAX_TILES, a, 0].reshape(span, HD), kv[MAX_TILES:RING, a, 0].reshape(span, HD)], axis=1
        )
        values = jnp.concatenate(
            [kv[0:MAX_TILES, a, 1].reshape(span, HD), kv[MAX_TILES:RING, a, 1].reshape(span, HD)], axis=1
        )
        keys_t = keys.T
        late = late_mask[...]
        for r in range(RATIO):
            cols = pl.ds(pl.multiple_of((a * RATIO + r) * HD, HD), HD)
            block = slice(r * 2 * tokens, (r + 1) * 2 * tokens)
            q = q_buf[:, :, cols].reshape(2 * tokens, HD)
            q_late = q * late
            qc = jnp.concatenate([q - q_late, q_late], axis=1)
            d = do_buf[:, :, cols].reshape(2 * tokens, HD)
            d_late = d * late
            dc = jnp.concatenate([d - d_late, d_late], axis=1)
            qc_all[block, :] = qc
            dc_all[block, :] = dc
            s = nt_dot(keys, qc)
            g = nt_dot(values, dc)
            s = jnp.concatenate(
                [s[t * tile:(t + 1) * tile] + biases[t] for t in range(MAX_TILES)], axis=0
            )
            top = jnp.max(s, axis=0, keepdims=True)
            e = jnp.exp2((s - top) * EXP2_SCALE)
            inv = 1.0 / jnp.sum(e, axis=0, keepdims=True)
            row_dot = jnp.sum(e * g, axis=0, keepdims=True) * inv
            p_all[:, block] = (e * inv).astype(BF16)
            ds = (e * ((g - row_dot) * (inv * SCALE))).astype(BF16)
            ds_all[:, block] = ds
            both = jnp.dot(keys_t, ds, preferred_element_type=F32)
            dq = jnp.where(early, both[:HD], both[HD:]).T.astype(BF16)
            dq_buf[:, :, cols] = dq.reshape(2, tokens, HD)
        dk = jnp.dot(ds_all[...], qc_all[...], preferred_element_type=F32)
        dv = jnp.dot(p_all[...], dc_all[...], preferred_element_type=F32)
        for sample in range(SAMP):
            for t in range(MAX_TILES):
                window = (slice(t * tile, (t + 1) * tile), slice(sample * HD, (sample + 1) * HD))
                part[a, sample * MAX_TILES + t, 0] = dk[window]
                part[a, sample * MAX_TILES + t, 1] = dv[window]
        rs_first(a)

        @pl.when(a >= 2)
        def _():
            rs_second(a - 2, 0)

        return carry

    lax.fori_loop(0, HALF_KV, head, 0)

    dq_keep = pltpu.make_async_copy(dq_buf.at[core], dq_ref.at[:, mine], dq_sem)
    dq_keep.start()
    dq_swap = remote(dq_buf.at[other], dq_ref.at[:, mine], dq_send, dq_recv, twin, enc)
    dq_swap.start()

    rs_second(2, 1)
    rs_second(3, 1)

    for a in range(HALF_KV):
        total = part[a, y]
        for way in range(2):
            for kind in (2, 3):
                rs_copy(way, kind, a, along[way][0]).wait_recv()
                total = total + rs_recv[way, kind, a].astype(F32)
        for kind in range(2):
            rows[pl.ds(kind * HALF_KV + a, tile, stride=2 * HALF_KV), :] = total[kind]

    pltpu.make_async_copy(slots.at[pl.ds(0, tile - 1)], slots.at[pl.ds(0, tile - 1)], in_send).wait()
    slots[...] = rows[...].reshape(slots.shape).astype(BF16)
    def scatter_out(i, carry):
        peer = peer_of(n_enc, enc, i)
        remote(slots.at[peer], dkv_ref.at[enc, core], out_send, out_recv, 2 * y, peer).start()
        remote(slots.at[n_enc + peer], dkv_ref.at[enc, core], out_send, out_recv, 2 * y + 1, peer).start()
        return carry

    lax.fori_loop(0, n_enc - 1, scatter_out, 0)

    keep_out = pltpu.make_async_copy(slots.at[here], dkv_ref.at[enc, core], out_recv)
    keep_out.start()
    remote(
        slots.at[other * n_enc + enc], dkv_ref.at[enc, core], out_send, out_recv, twin, enc
    ).start()

    for swap in swaps:
        swap.wait_send()

    def drain(a, carry):
        for way in range(2):
            ag_copy(way, a, 0, 1).wait_send()
            ag_copy(way, a, 0, 2).wait_send()
            ag_copy(way, a, 2, 1).wait_send()
            for kind in (0, 2, 3):
                rs_copy(way, kind, a, along[way][0]).wait_send()
        far_copy(a).wait_send()
        rs_copy(a // 2, 1, a, along[0][0]).wait_send()
        return carry

    lax.fori_loop(0, HALF_KV, drain, 0)
    dq_keep.wait()
    dq_swap.wait()
    pltpu.make_async_copy(slots.at[pl.ds(0, tile - 1)], slots.at[pl.ds(0, tile - 1)], out_send).wait()
    pltpu.make_async_copy(dkv_ref, dkv_ref, out_recv).wait()


def finish(n_enc, dq_ref, dkv_ref, dq_out, k_out, v_out, rows, sem):
    keep = pltpu.make_async_copy(dq_ref, dq_out, sem)
    keep.start()
    rows[...] = dkv_ref[...].astype(F32).reshape(rows.shape)
    for kind, out in enumerate((k_out, v_out)):
        for h in range(KVH):
            first = h // HALF_KV * 2 * HALF_KV + kind * HALF_KV + h % HALF_KV
            out[:, h * HD:(h + 1) * HD] = rows[pl.ds(first, n_enc, stride=4 * HALF_KV), :].astype(BF16)
    keep.wait()


def shards(n_enc, queries, d_out, text_sample, tiles, img_k, img_v):
    tokens, width = queries.shape[1:]
    tile = 2 * n_enc
    span = MAX_TILES * tile
    rows = HALF_KV * 2
    vmem = pl.BlockSpec(memory_space=pltpu.VMEM)
    anywhere = pl.BlockSpec(memory_space=pl.ANY)
    dma = pltpu.SemaphoreType.DMA
    d_queries, d_own = pl.pallas_call(
        functools.partial(kernel, n_enc),
        out_shape=(
            pltpu.VMEM((tokens, width), BF16),
            pltpu.VMEM((n_enc, 2, rows, HD), BF16),
        ),
        in_specs=[anywhere] * 6,
        out_specs=(anywhere, anywhere),
        scratch_shapes=[
            pltpu.SMEM((1, SAMP), jnp.int32),
            pltpu.VMEM((2, 1, tokens), jnp.int32),
            pltpu.VMEM((2, n_enc, KVH * HD), BF16),
            pltpu.VMEM((n_enc, 2, rows, HD), BF16),
            pltpu.VMEM((2 * tokens, HD), BF16),
            pltpu.VMEM((2, tokens, width // 2), BF16),
            pltpu.VMEM((2, tokens, width // 2), BF16),
            pltpu.VMEM((2, tokens, width // 2), BF16),
            pltpu.VMEM((tile, rows, HD), BF16),
            pltpu.VMEM((tile * rows, HD), F32),
            pltpu.VMEM((RING, HALF_KV, 2, tile, HD), BF16),
            pltpu.VMEM((span, RATIO * 2 * tokens), BF16),
            pltpu.VMEM((span, RATIO * 2 * tokens), BF16),
            pltpu.VMEM((RATIO * 2 * tokens, 2 * HD), BF16),
            pltpu.VMEM((RATIO * 2 * tokens, 2 * HD), BF16),
            pltpu.VMEM((HALF_KV, RING, 2, tile, HD), F32),
            pltpu.VMEM((2, 4, HALF_KV, 2, tile, HD), BF16),
            pltpu.VMEM((2, 4, HALF_KV, 2, tile, HD), BF16),
            dma((2,)),
            dma((3,)),
            dma((3,)),
            dma,
            dma,
            dma((2, 4, HALF_KV)),
            dma((2, 4, HALF_KV)),
            dma((2, 4, HALF_KV)),
            dma((2, 4, HALF_KV)),
            dma,
            dma,
            dma,
            dma,
            dma,
            dma((4,)),
        ],
        compiler_params=pltpu.CompilerParams(
            collective_id=0, has_side_effects=True, vmem_limit_bytes=VMEM_LIMIT
        ),
    )(
        tiles,
        text_sample,
        img_k.reshape(n_enc, KVH * HD),
        img_v.reshape(n_enc, KVH * HD),
        queries[0],
        d_out[0],
    )
    d_queries, back_keys, back_values = pl.pallas_call(
        functools.partial(finish, n_enc),
        out_shape=(
            jax.ShapeDtypeStruct((tokens, width), BF16),
            jax.ShapeDtypeStruct((n_enc, KVH * HD), BF16),
            jax.ShapeDtypeStruct((n_enc, KVH * HD), BF16),
        ),
        in_specs=[vmem, vmem],
        out_specs=(anywhere, vmem, vmem),
        scratch_shapes=[
            pltpu.VMEM((n_enc * 2 * rows, HD), F32),
            dma,
        ],
        compiler_params=pltpu.CompilerParams(vmem_limit_bytes=VMEM_LIMIT // 4),
    )(d_queries, d_own)
    return (
        d_queries[None],
        back_keys.reshape(n_enc, 1, KVH * HD),
        back_values.reshape(n_enc, 1, KVH * HD),
    )


def solution(mesh):
    in_specs = (
        P("enc", "ctx", None),
        P("enc", "ctx", None),
        P("enc", "ctx"),
        P("enc", None),
        P(None, ("ctx", "enc"), None),
        P(None, ("ctx", "enc"), None),
    )
    out_specs = (
        P("enc", "ctx", None),
        P(None, ("ctx", "enc"), None),
        P(None, ("ctx", "enc"), None),
    )
    return jax.shard_map(
        functools.partial(shards, mesh.shape["enc"]),
        mesh=mesh,
        in_specs=in_specs,
        out_specs=out_specs,
        check_vma=False,
    )
```

time: 76.5 us -> 64.5 us (0.84)
  local copies, waits for them, and re-layouts: 6.3 us -> 0 us
  Pallas kernels: 69.2 us -> 63.8 us
    pallas_call x1 -> x2, Pallas kernels: 69.2 us -> 63.8 us  [the longest x1 62.1 us: shards(): pl.pallas_call(functools.partial(kernel, n_enc), out_shape=(pltpu.VMEM((t...]
    unnamed x11 -> x0, local copies, waits for them, and re-layouts: 4 us -> none
    reshape x4 -> x0, local copies, waits for them, and re-layouts: 2.26 us -> none  [the longest x1 0.9 us: shards(): img_k.reshape(n_enc, 2, HALF_KV, HD)]
where the time goes in v2:
time: 64.5 us; the launch traced here: 64.4 us
  Pallas kernels  63.8 us (99%)
    pallas_call x1, Pallas kernels, shards(): pl.pallas_call(functools.partial(kernel, n_enc), out_shape=(pltpu.VMEM((t...  62.1 us
    pallas_call x1, Pallas kernels, shards(): pl.pallas_call(functools.partial(finish, n_enc), out_shape=(jax.ShapeDtyp...  1.63 us

profile of v2, /device:TPU:1, one launch (start us, length us, event | category | flops | bytes accessed | tf_op | source)
XLA Modules:
  0.0 64.4 jit_solution(4371178215551975793)
XLA Ops:
  0.6 62.1 %shard_map.85 = (bf16[128,4096]{1,0:T(8,128)(2,1)S(1)}, bf16[32,2,8,128]{3,2,1,0:T(8,128)(2,1)S(1)}) custom-call(s32[1,2]{1,0:T(1,128)} %tiles_hbm.1, s32[1,128]{1,0:T(1,128)} %text_hbm.1, bf16[32,1024]{1,0:T(8,128)(2,1)} %bitcast.9, bf16[32,1024]{1,0:T(8,128)(2,1)} %bitcast.10, bf16[128,4096]{1,0:T(8,128)(2,1)} %bitcast.7, bf16[128,4096]{1,0:T(8,128)(2,1)} %bitcast.8), custom_call_target="tpu_custom_call" | custom-call | tf_op jit(solution)/shard_map/pallas_call | solution.py:397
  62.8 1.6 %shard_map.86 = (bf16[128,4096]{1,0:T(8,128)(2,1)}, bf16[32,1024]{1,0:T(8,128)(2,1)}, bf16[32,1024]{1,0:T(8,128)(2,1)}) custom-call(bf16[128,4096]{1,0:T(8,128)(2,1)S(1)} %get-tuple-element.8.dq_ref, bf16[32,2,8,128]{3,2,1,0:T(8,128)(2,1)S(1)} %get-tuple-element.9.dkv_ref), custom_call_target="tpu_custom_call" | custom-call | tf_op jit(solution)/shard_map/pallas_call | solution.py:451

commit v3 on v2

--- a/solution.py
+++ b/solution.py
@@ -21,6 +21,7 @@
 
 big_negative = -1e30
 VMEM_LIMIT = 58 * 1024 * 1024
+LONG_FROM = 2
 
 MESH = pl.DeviceIdType.MESH
 F32 = jnp.float32
@@ -38,15 +39,23 @@
     )
 
 
-def peer_of(n_enc, enc, i):
-    if n_enc != 32:
-        return lax.rem(enc + i + 1, n_enc)
-    far_z = i // 4
-    near = (far_z + 1) // 2
-    z = lax.rem(enc // 4 + 12 + near - 2 * near * lax.rem(far_z + 1, 2), 8)
-    far_x = lax.rem(i, 4)
-    x = lax.rem(enc + 2 + far_x + far_x // 2 * (1 - 2 * lax.rem(far_x, 2)), 4)
-    return 4 * z + x
+def each_peer(n_enc, enc, visit):
+    n_x = min(4, n_enc)
+    n_z = n_enc // n_x
+    z, x = enc // n_x, lax.rem(enc, n_x)
+    columns = [lax.rem(x + step, n_x) for step in sorted(range(1, n_x), key=lambda step: -min(step, n_x - step))]
+
+    def plane(i, carry):
+        near = (i + 1) // 2
+        row = lax.rem(z + n_z + n_z // 2 + near - 2 * near * lax.rem(i + 1, 2), n_z) * n_x
+        for column in columns + [x]:
+            visit(row + column)
+        return carry
+
+    if n_z > 1:
+        lax.fori_loop(0, n_z - 1, plane, 0)
+    for column in columns:
+        visit(z * n_x + column)
 
 
 def nt_dot(a, b):
@@ -74,8 +83,9 @@
     slots,
     rows,
     kv,
+    scores,
+    grads,
     ds_all,
-    p_all,
     qc_all,
     dc_all,
     part,
@@ -114,19 +124,6 @@
     mine = pl.ds(pl.multiple_of(core * width, width), width)
     theirs = pl.ds(pl.multiple_of(other * width, width), width)
 
-    barrier = pltpu.get_barrier_semaphore()
-    pl.semaphore_signal(barrier, inc=1, device_id=(twin, enc), device_id_type=MESH)
-    for step in range(2):
-        pl.semaphore_signal(barrier, inc=1, device_id=(ahead[step], enc), device_id_type=MESH)
-        pl.semaphore_signal(barrier, inc=1, device_id=(behind[step], enc), device_id_type=MESH)
-
-    def greet(i, carry):
-        peer = peer_of(n_enc, enc, i)
-        pl.semaphore_signal(barrier, inc=1, device_id=(2 * y, peer), device_id_type=MESH)
-        pl.semaphore_signal(barrier, inc=1, device_id=(2 * y + 1, peer), device_id_type=MESH)
-        return carry
-
-    lax.fori_loop(0, n_enc - 1, greet, 0)
     load_k = pltpu.make_async_copy(k_ref, kv_in.at[0], small_sem.at[0])
     load_v = pltpu.make_async_copy(v_ref, kv_in.at[1], small_sem.at[1])
     load_tiles = pltpu.make_async_copy(tiles_hbm, tiles_ref, small_sem.at[2])
@@ -137,6 +134,18 @@
     for load in loads:
         load.start()
 
+    barrier = pltpu.get_barrier_semaphore()
+    pl.semaphore_signal(barrier, inc=1, device_id=(twin, enc), device_id_type=MESH)
+    for step in range(2):
+        pl.semaphore_signal(barrier, inc=1, device_id=(ahead[step], enc), device_id_type=MESH)
+        pl.semaphore_signal(barrier, inc=1, device_id=(behind[step], enc), device_id_type=MESH)
+
+    def greet(peer):
+        pl.semaphore_signal(barrier, inc=1, device_id=(2 * y, peer), device_id_type=MESH)
+        pl.semaphore_signal(barrier, inc=1, device_id=(2 * y + 1, peer), device_id_type=MESH)
+
+    each_peer(n_enc, enc, greet)
+
     load_k.wait()
     load_v.wait()
     for kind in range(2):
@@ -149,14 +158,11 @@
     pl.semaphore_wait(barrier, 2 * n_enc + 3)
 
     here = core * n_enc + enc
-    def scatter_in(i, carry):
-        peer = peer_of(n_enc, enc, i)
+    def scatter_in(peer):
         remote(own_ref.at[peer, 0], slots.at[here], in_send, in_recv, 2 * y, peer).start()
         remote(own_ref.at[peer, 1], slots.at[here], in_send, in_recv, 2 * y + 1, peer).start()
-        return carry
-
-    lax.fori_loop(0, n_enc - 1, scatter_in, 0)
-
+
+    each_peer(n_enc, enc, scatter_in)
     keep_in = pltpu.make_async_copy(own_ref.at[enc, core], slots.at[here], in_recv)
     keep_in.start()
     remote(own_ref.at[enc, other], slots.at[here], in_send, in_recv, twin, enc).start()
@@ -190,14 +196,12 @@
             kv.at[block, a], kv.at[block, a], ag_send.at[way, sem, a], ag_recv.at[way, sem, a], along[way][0], enc
         ).wait_recv()
 
-    for step in (2, 1):
-
-        def ag_first(a, carry, step=step):
-            ag_copy(0, a, 0, step).start()
-            ag_copy(1, a, 0, step).start()
-            return carry
-
-        lax.fori_loop(0, HALF_KV, ag_first, 0)
+    def ag_first(a, carry):
+        ag_copy(0, a, 0, 1).start()
+        ag_copy(1, a, 0, 1).start()
+        return carry
+
+    lax.fori_loop(0, HALF_KV, ag_first, 0)
 
     load_tiles.wait()
     load_text.wait()
@@ -212,6 +216,10 @@
 
     for a in range(HALF_KV):
         for way in range(2):
+            ag_wait(way, a, 1)
+            ag_copy(way, a, 1, 1).start()
+    for a in range(HALF_KV):
+        for way in range(2):
             ag_wait(way, a, 2)
             if way == a // 2:
                 ag_copy(way, a, 2, 2).start()
@@ -221,6 +229,18 @@
     load_do.wait()
     swaps[1].wait_recv()
     swaps[2].wait_recv()
+
+    def spread_heads(h, carry):
+        cols = pl.ds(pl.multiple_of(h * HD, HD), HD)
+        late = late_mask[...]
+        for source, target in ((q_buf, qc_all), (do_buf, dc_all)):
+            every = source[:, :, cols].reshape(2 * tokens, HD)
+            second = every * late
+            target[h, :, :HD] = every - second
+            target[h, :, HD:] = second
+        return carry
+
+    lax.fori_loop(0, HALF_KV * RATIO, spread_heads, 0)
 
     far = lax.rem(y + 4, RING)
 
@@ -250,11 +270,14 @@
         for way in range(2):
             rs_send[way, 0, a] = part[a, due(way, 3)].astype(BF16)
             rs_copy(way, 0, a, along[way][0]).start()
-        for way in range(2):
-            rs_send[way, 2, a] = part[a, due(way, 1)].astype(BF16)
-            rs_copy(way, 2, a, along[way][0]).start()
-
-    def rs_second(a, side):
+
+        @pl.when(a >= LONG_FROM)
+        def _():
+            for way in range(2):
+                rs_send[way, 2, a] = part[a, due(way, 1)].astype(BF16)
+                rs_copy(way, 2, a, along[way][0]).start()
+
+    def rs_second(a, side, steps):
         for way in range(2):
             total = part[a, due(way, 2)]
             rs_copy(way, 0, a, along[way][0]).wait_recv()
@@ -263,11 +286,17 @@
                 rs_copy(way, 1, a, along[way][0]).wait_recv()
                 total = total + rs_recv[way, 1, a].astype(F32)
             rs_send[way, 3, a] = total.astype(BF16)
-            rs_copy(way, 3, a, along[way][1]).start()
+            rs_copy(way, 3, a, along[way][steps - 1]).start()
+
+    def rs_third(a):
+        for way in range(2):
+            rs_copy(way, 3, a, along[way][0]).wait_recv()
+            total = part[a, due(way, 1)] + rs_recv[way, 3, a].astype(F32)
+            rs_send[way, 2, a] = total.astype(BF16)
+            rs_copy(way, 2, a, along[way][0]).start()
 
     def head(a, carry):
         for way in range(2):
-            ag_wait(way, a, 1)
             ag_wait(way, a, 3)
         far_copy(a).wait_recv()
         keys = jnp.concatenate(
@@ -276,21 +305,14 @@
         values = jnp.concatenate(
             [kv[0:MAX_TILES, a, 1].reshape(span, HD), kv[MAX_TILES:RING, a, 1].reshape(span, HD)], axis=1
         )
-        keys_t = keys.T
-        late = late_mask[...]
         for r in range(RATIO):
-            cols = pl.ds(pl.multiple_of((a * RATIO + r) * HD, HD), HD)
-            block = slice(r * 2 * tokens, (r + 1) * 2 * tokens)
-            q = q_buf[:, :, cols].reshape(2 * tokens, HD)
-            q_late = q * late
-            qc = jnp.concatenate([q - q_late, q_late], axis=1)
-            d = do_buf[:, :, cols].reshape(2 * tokens, HD)
-            d_late = d * late
-            dc = jnp.concatenate([d - d_late, d_late], axis=1)
-            qc_all[block, :] = qc
-            dc_all[block, :] = dc
-            s = nt_dot(keys, qc)
-            g = nt_dot(values, dc)
+            scores[r] = nt_dot(keys, qc_all[a * RATIO + r])
+            grads[r] = nt_dot(values, dc_all[a * RATIO + r])
+        dk = jnp.zeros((span, 2 * HD), F32)
+        dv = jnp.zeros((span, 2 * HD), F32)
+        for r in range(RATIO):
+            s = scores[r]
+            g = grads[r]
             s = jnp.concatenate(
                 [s[t * tile:(t + 1) * tile] + biases[t] for t in range(MAX_TILES)], axis=0
             )
@@ -298,14 +320,11 @@
             e = jnp.exp2((s - top) * EXP2_SCALE)
             inv = 1.0 / jnp.sum(e, axis=0, keepdims=True)
             row_dot = jnp.sum(e * g, axis=0, keepdims=True) * inv
-            p_all[:, block] = (e * inv).astype(BF16)
+            p = (e * inv).astype(BF16)
             ds = (e * ((g - row_dot) * (inv * SCALE))).astype(BF16)
-            ds_all[:, block] = ds
-            both = jnp.dot(keys_t, ds, preferred_element_type=F32)
-            dq = jnp.where(early, both[:HD], both[HD:]).T.astype(BF16)
-            dq_buf[:, :, cols] = dq.reshape(2, tokens, HD)
-        dk = jnp.dot(ds_all[...], qc_all[...], preferred_element_type=F32)
-        dv = jnp.dot(p_all[...], dc_all[...], preferred_element_type=F32)
+            ds_all[a * RATIO + r] = ds
+            dk = dk + jnp.dot(ds, qc_all[a * RATIO + r], preferred_element_type=F32)
+            dv = dv + jnp.dot(p, dc_all[a * RATIO + r], preferred_element_type=F32)
         for sample in range(SAMP):
             for t in range(MAX_TILES):
                 window = (slice(t * tile, (t + 1) * tile), slice(sample * HD, (sample + 1) * HD))
@@ -315,24 +334,40 @@
 
         @pl.when(a >= 2)
         def _():
-            rs_second(a - 2, 0)
+            rs_second(a - 2, 0, 1)
 
         return carry
 
     lax.fori_loop(0, HALF_KV, head, 0)
 
+    def query_grads(a, carry):
+        keys_t = jnp.concatenate(
+            [kv[0:MAX_TILES, a, 0].reshape(span, HD), kv[MAX_TILES:RING, a, 0].reshape(span, HD)], axis=1
+        ).T
+        for r in range(RATIO):
+            cols = pl.ds(pl.multiple_of((a * RATIO + r) * HD, HD), HD)
+            both = jnp.dot(keys_t, ds_all[a * RATIO + r], preferred_element_type=F32)
+            dq = jnp.where(early, both[:HD], both[HD:]).T.astype(BF16)
+            dq_buf[:, :, cols] = dq.reshape(2, tokens, HD)
+        return carry
+
+    lax.fori_loop(0, HALF_KV // 2, query_grads, 0)
+    rs_second(2, 1, 1 if LONG_FROM > 2 else 2)
+    rs_third(0)
+    lax.fori_loop(HALF_KV // 2, HALF_KV, query_grads, 0)
+    rs_second(3, 1, 1 if LONG_FROM > 3 else 2)
+    rs_third(1)
+    for a in range(2, LONG_FROM):
+        rs_third(a)
     dq_keep = pltpu.make_async_copy(dq_buf.at[core], dq_ref.at[:, mine], dq_sem)
     dq_keep.start()
     dq_swap = remote(dq_buf.at[other], dq_ref.at[:, mine], dq_send, dq_recv, twin, enc)
     dq_swap.start()
 
-    rs_second(2, 1)
-    rs_second(3, 1)
-
     for a in range(HALF_KV):
         total = part[a, y]
         for way in range(2):
-            for kind in (2, 3):
+            for kind in (2, 3) if a >= LONG_FROM else (2,):
                 rs_copy(way, kind, a, along[way][0]).wait_recv()
                 total = total + rs_recv[way, kind, a].astype(F32)
         for kind in range(2):
@@ -340,14 +375,11 @@
 
     pltpu.make_async_copy(slots.at[pl.ds(0, tile - 1)], slots.at[pl.ds(0, tile - 1)], in_send).wait()
     slots[...] = rows[...].reshape(slots.shape).astype(BF16)
-    def scatter_out(i, carry):
-        peer = peer_of(n_enc, enc, i)
+    def scatter_out(peer):
         remote(slots.at[peer], dkv_ref.at[enc, core], out_send, out_recv, 2 * y, peer).start()
         remote(slots.at[n_enc + peer], dkv_ref.at[enc, core], out_send, out_recv, 2 * y + 1, peer).start()
-        return carry
-
-    lax.fori_loop(0, n_enc - 1, scatter_out, 0)
-
+
+    each_peer(n_enc, enc, scatter_out)
     keep_out = pltpu.make_async_copy(slots.at[here], dkv_ref.at[enc, core], out_recv)
     keep_out.start()
     remote(
@@ -375,15 +407,23 @@
     pltpu.make_async_copy(dkv_ref, dkv_ref, out_recv).wait()
 
 
-def finish(n_enc, dq_ref, dkv_ref, dq_out, k_out, v_out, rows, sem):
-    keep = pltpu.make_async_copy(dq_ref, dq_out, sem)
-    keep.start()
+def finish(n_enc, dq_ref, dkv_ref, dq_out, k_out, v_out, rows, k_rows, v_rows, sem):
+    half = dq_ref.shape[0] // 2
+    copies = [
+        pltpu.make_async_copy(dq_ref.at[pl.ds(i * half, half)], dq_out.at[pl.ds(i * half, half)], sem.at[i])
+        for i in range(2)
+    ]
+    for copy in copies:
+        copy.start()
     rows[...] = dkv_ref[...].astype(F32).reshape(rows.shape)
-    for kind, out in enumerate((k_out, v_out)):
+    for kind, (lines, out) in enumerate(((k_rows, k_out), (v_rows, v_out))):
         for h in range(KVH):
             first = h // HALF_KV * 2 * HALF_KV + kind * HALF_KV + h % HALF_KV
-            out[:, h * HD:(h + 1) * HD] = rows[pl.ds(first, n_enc, stride=4 * HALF_KV), :].astype(BF16)
-    keep.wait()
+            lines[:, h * HD:(h + 1) * HD] = rows[pl.ds(first, n_enc, stride=4 * HALF_KV), :].astype(BF16)
+        copies.append(pltpu.make_async_copy(lines, out, sem.at[2 + kind]))
+        copies[-1].start()
+    for copy in copies:
+        copy.wait()
 
 
 def shards(n_enc, queries, d_out, text_sample, tiles, img_k, img_v):
@@ -414,10 +454,11 @@
             pltpu.VMEM((tile, rows, HD), BF16),
             pltpu.VMEM((tile * rows, HD), F32),
             pltpu.VMEM((RING, HALF_KV, 2, tile, HD), BF16),
-            pltpu.VMEM((span, RATIO * 2 * tokens), BF16),
-            pltpu.VMEM((span, RATIO * 2 * tokens), BF16),
-            pltpu.VMEM((RATIO * 2 * tokens, 2 * HD), BF16),
-            pltpu.VMEM((RATIO * 2 * tokens, 2 * HD), BF16),
+            pltpu.VMEM((RATIO, span, 2 * tokens), F32),
+            pltpu.VMEM((RATIO, span, 2 * tokens), F32),
+            pltpu.VMEM((HALF_KV * RATIO, span, 2 * tokens), BF16),
+            pltpu.VMEM((HALF_KV * RATIO, 2 * tokens, 2 * HD), BF16),
+            pltpu.VMEM((HALF_KV * RATIO, 2 * tokens, 2 * HD), BF16),
             pltpu.VMEM((HALF_KV, RING, 2, tile, HD), F32),
             pltpu.VMEM((2, 4, HALF_KV, 2, tile, HD), BF16),
             pltpu.VMEM((2, 4, HALF_KV, 2, tile, HD), BF16),
@@ -456,10 +497,12 @@
             jax.ShapeDtypeStruct((n_enc, KVH * HD), BF16),
         ),
         in_specs=[vmem, vmem],
-        out_specs=(anywhere, vmem, vmem),
+        out_specs=(anywhere, anywhere, anywhere),
         scratch_shapes=[
             pltpu.VMEM((n_enc * 2 * rows, HD), F32),
-            dma,
+            pltpu.VMEM((n_enc, KVH * HD), BF16),
+            pltpu.VMEM((n_enc, KVH * HD), BF16),
+            dma((4,)),
         ],
         compiler_params=pltpu.CompilerParams(vmem_limit_bytes=VMEM_LIMIT // 4),
     )(d_queries, d_own)

time: 64.5 us -> 60.5 us (0.938)
  Pallas kernels: 63.8 us -> 59.7 us
    pallas_call x1, Pallas kernels: 62.1 us -> 58.7 us  [shards(): pl.pallas_call(functools.partial(kernel, n_enc), out_shape=(pltpu.VMEM((t...]
where the time goes in v3:
time: 60.5 us; the launch traced here: 60.3 us
  Pallas kernels  59.7 us (99%)
  between operations  0.64 us (1%)
    pallas_call x1, Pallas kernels, shards(): pl.pallas_call(functools.partial(kernel, n_enc), out_shape=(pltpu.VMEM((t...  58.7 us

profile of v3, /device:TPU:1, one launch (start us, length us, event | category | flops | bytes accessed | tf_op | source)
XLA Modules:
  0.0 60.3 jit_solution(12236243180932941189)
XLA Ops:
  0.6 58.7 %shard_map.85 = (bf16[128,4096]{1,0:T(8,128)(2,1)S(1)}, bf16[32,2,8,128]{3,2,1,0:T(8,128)(2,1)S(1)}) custom-call(s32[1,2]{1,0:T(1,128)} %tiles_hbm.1, s32[1,128]{1,0:T(1,128)} %text_hbm.1, bf16[32,1024]{1,0:T(8,128)(2,1)} %bitcast.9, bf16[32,1024]{1,0:T(8,128)(2,1)} %bitcast.10, bf16[128,4096]{1,0:T(8,128)(2,1)} %bitcast.7, bf16[128,4096]{1,0:T(8,128)(2,1)} %bitcast.8), custom_call_target="tpu_custom_call" | custom-call | tf_op jit(solution)/shard_map/pallas_call | solution.py:437
  59.3 1.0 %shard_map.86 = (bf16[128,4096]{1,0:T(8,128)(2,1)}, bf16[32,1024]{1,0:T(8,128)(2,1)}, bf16[32,1024]{1,0:T(8,128)(2,1)}) custom-call(bf16[128,4096]{1,0:T(8,128)(2,1)S(1)} %get-tuple-element.8.dq_ref, bf16[32,2,8,128]{3,2,1,0:T(8,128)(2,1)S(1)} %get-tuple-element.9.dkv_ref), custom_call_target="tpu_custom_call" | custom-call | tf_op jit(solution)/shard_map/pallas_call | solution.py:492

commit v4 on v3

--- a/solution.py
+++ b/solution.py
@@ -21,7 +21,7 @@
 
 big_negative = -1e30
 VMEM_LIMIT = 58 * 1024 * 1024
-LONG_FROM = 2
+LONG_FROM = 3
 
 MESH = pl.DeviceIdType.MESH
 F32 = jnp.float32
@@ -56,6 +56,10 @@
         lax.fori_loop(0, n_z - 1, plane, 0)
     for column in columns:
         visit(z * n_x + column)
+
+
+def side_of(a):
+    return a % 2 if isinstance(a, int) else lax.rem(a, 2)
 
 
 def nt_dot(a, b):
@@ -221,7 +225,7 @@
     for a in range(HALF_KV):
         for way in range(2):
             ag_wait(way, a, 2)
-            if way == a // 2:
+            if way == side_of(a):
                 ag_copy(way, a, 2, 2).start()
             ag_copy(way, a, 2, 1).start()
 
@@ -245,7 +249,7 @@
     far = lax.rem(y + 4, RING)
 
     def far_copy(a):
-        side = a // 2
+        side = side_of(a)
         return remote(
             kv.at[far, a], kv.at[far, a], ag_send.at[side, 3, a], ag_recv.at[side, 3, a], along[0][0], enc
         )
@@ -264,7 +268,7 @@
         return lax.rem(y + steps, RING) if way == 0 else lax.rem(y + RING - steps, RING)
 
     def rs_first(a):
-        side = a // 2
+        side = side_of(a)
         rs_send[side, 1, a] = part[a, far].astype(BF16)
         rs_copy(side, 1, a, ahead[1] + side * (behind[1] - ahead[1])).start()
         for way in range(2):
@@ -277,7 +281,9 @@
                 rs_send[way, 2, a] = part[a, due(way, 1)].astype(BF16)
                 rs_copy(way, 2, a, along[way][0]).start()
 
-    def rs_second(a, side, steps):
+    def rs_second(a):
+        side = side_of(a)
+        steps = 1 if a < LONG_FROM else 2
         for way in range(2):
             total = part[a, due(way, 2)]
             rs_copy(way, 0, a, along[way][0]).wait_recv()
@@ -332,10 +338,6 @@
                 part[a, sample * MAX_TILES + t, 1] = dv[window]
         rs_first(a)
 
-        @pl.when(a >= 2)
-        def _():
-            rs_second(a - 2, 0, 1)
-
         return carry
 
     lax.fori_loop(0, HALF_KV, head, 0)
@@ -352,13 +354,15 @@
         return carry
 
     lax.fori_loop(0, HALF_KV // 2, query_grads, 0)
-    rs_second(2, 1, 1 if LONG_FROM > 2 else 2)
+    rs_second(0)
+    rs_second(1)
+    lax.fori_loop(HALF_KV // 2, HALF_KV, query_grads, 0)
+    rs_second(2)
     rs_third(0)
-    lax.fori_loop(HALF_KV // 2, HALF_KV, query_grads, 0)
-    rs_second(3, 1, 1 if LONG_FROM > 3 else 2)
+    rs_second(3)
     rs_third(1)
-    for a in range(2, LONG_FROM):
-        rs_third(a)
+    rs_third(2)
+
     dq_keep = pltpu.make_async_copy(dq_buf.at[core], dq_ref.at[:, mine], dq_sem)
     dq_keep.start()
     dq_swap = remote(dq_buf.at[other], dq_ref.at[:, mine], dq_send, dq_recv, twin, enc)
@@ -397,7 +401,7 @@
             for kind in (0, 2, 3):
                 rs_copy(way, kind, a, along[way][0]).wait_send()
         far_copy(a).wait_send()
-        rs_copy(a // 2, 1, a, along[0][0]).wait_send()
+        rs_copy(side_of(a), 1, a, along[0][0]).wait_send()
         return carry
 
     lax.fori_loop(0, HALF_KV, drain, 0)

time: 60.5 us -> 59.5 us (0.983)
  Pallas kernels: 59.7 us -> 58.7 us
    pallas_call x1, Pallas kernels: 58.7 us -> 57.7 us  [shards(): pl.pallas_call(functools.partial(kernel, n_enc), out_shape=(pltpu.VMEM((t...]
where the time goes in v4:
time: 59.5 us; the launch traced here: 59.4 us
  Pallas kernels  58.7 us (99%)
  between operations  0.64 us (1%)
    pallas_call x1, Pallas kernels, shards(): pl.pallas_call(functools.partial(kernel, n_enc), out_shape=(pltpu.VMEM((t...  57.7 us

profile of v4, /device:TPU:1, one launch (start us, length us, event | category | flops | bytes accessed | tf_op | source)
XLA Modules:
  0.0 59.4 jit_solution(16679346904862275548)
XLA Ops:
  0.6 57.7 %shard_map.85 = (bf16[128,4096]{1,0:T(8,128)(2,1)S(1)}, bf16[32,2,8,128]{3,2,1,0:T(8,128)(2,1)S(1)}) custom-call(s32[1,2]{1,0:T(1,128)} %tiles_hbm.1, s32[1,128]{1,0:T(1,128)} %text_hbm.1, bf16[32,1024]{1,0:T(8,128)(2,1)} %bitcast.9, bf16[32,1024]{1,0:T(8,128)(2,1)} %bitcast.10, bf16[128,4096]{1,0:T(8,128)(2,1)} %bitcast.7, bf16[128,4096]{1,0:T(8,128)(2,1)} %bitcast.8), custom_call_target="tpu_custom_call" | custom-call | tf_op jit(solution)/shard_map/pallas_call | solution.py:441
  58.3 1.0 %shard_map.86 = (bf16[128,4096]{1,0:T(8,128)(2,1)}, bf16[32,1024]{1,0:T(8,128)(2,1)}, bf16[32,1024]{1,0:T(8,128)(2,1)}) custom-call(bf16[128,4096]{1,0:T(8,128)(2,1)S(1)} %get-tuple-element.8.dq_ref, bf16[32,2,8,128]{3,2,1,0:T(8,128)(2,1)S(1)} %get-tuple-element.9.dkv_ref), custom_call_target="tpu_custom_call" | custom-call | tf_op jit(solution)/shard_map/pallas_call | solution.py:496

commit v5 on v4

--- a/solution.py
+++ b/solution.py
@@ -181,10 +181,6 @@
 
     pltpu.make_async_copy(slots, slots, in_recv).wait()
     rows[...] = slots[...].astype(F32).reshape(rows.shape)
-    for kind in range(2):
-        for a in range(HALF_KV):
-            lines = rows[pl.ds(kind * HALF_KV + a, tile, stride=2 * HALF_KV), :]
-            kv[y, a, kind] = lines.astype(BF16)
 
     def ag_copy(way, a, offset, step):
         block = lax.rem(y + RING - offset, RING) if way == 0 else lax.rem(y + offset, RING)
@@ -200,12 +196,12 @@
             kv.at[block, a], kv.at[block, a], ag_send.at[way, sem, a], ag_recv.at[way, sem, a], along[way][0], enc
         ).wait_recv()
 
-    def ag_first(a, carry):
+    for a in range(HALF_KV):
+        for kind in range(2):
+            lines = rows[pl.ds(kind * HALF_KV + a, tile, stride=2 * HALF_KV), :]
+            kv[y, a, kind] = lines.astype(BF16)
         ag_copy(0, a, 0, 1).start()
         ag_copy(1, a, 0, 1).start()
-        return carry
-
-    lax.fori_loop(0, HALF_KV, ag_first, 0)
 
     load_tiles.wait()
     load_text.wait()

time: 59.5 us -> 59.5 us (level)
  no operation moved by 1% of the time
where the time goes in v5:
time: 59.5 us; the launch traced here: 59.3 us
  Pallas kernels  58.7 us (99%)
  between operations  0.64 us (1%)
    pallas_call x1, Pallas kernels, shards(): pl.pallas_call(functools.partial(kernel, n_enc), out_shape=(pltpu.VMEM((t...  57.6 us

profile of v5, /device:TPU:1, one launch (start us, length us, event | category | flops | bytes accessed | tf_op | source)
XLA Modules:
  0.0 59.3 jit_solution(12236750522239492912)
XLA Ops:
  0.6 57.6 %shard_map.85 = (bf16[128,4096]{1,0:T(8,128)(2,1)S(1)}, bf16[32,2,8,128]{3,2,1,0:T(8,128)(2,1)S(1)}) custom-call(s32[1,2]{1,0:T(1,128)} %tiles_hbm.1, s32[1,128]{1,0:T(1,128)} %text_hbm.1, bf16[32,1024]{1,0:T(8,128)(2,1)} %bitcast.9, bf16[32,1024]{1,0:T(8,128)(2,1)} %bitcast.10, bf16[128,4096]{1,0:T(8,128)(2,1)} %bitcast.7, bf16[128,4096]{1,0:T(8,128)(2,1)} %bitcast.8), custom_call_target="tpu_custom_call" | custom-call | tf_op jit(solution)/shard_map/pallas_call | solution.py:437
  58.3 1.0 %shard_map.86 = (bf16[128,4096]{1,0:T(8,128)(2,1)}, bf16[32,1024]{1,0:T(8,128)(2,1)}, bf16[32,1024]{1,0:T(8,128)(2,1)}) custom-call(bf16[128,4096]{1,0:T(8,128)(2,1)S(1)} %get-tuple-element.8.dq_ref, bf16[32,2,8,128]{3,2,1,0:T(8,128)(2,1)S(1)} %get-tuple-element.9.dkv_ref), custom_call_target="tpu_custom_call" | custom-call | tf_op jit(solution)/shard_map/pallas_call | solution.py:492
